TPU v7x, 32 devices: a whole 2x2x4 slice. The times are simulated.
32 devices in a mesh: groups: 2 (over y), inst: 4 (over x, core), tp: 4 (over z).
Axes of the slice: x: 2, y: 2, z: 4, core: 2. Of those that a mesh axis runs over, the one named last changes fastest.
Arguments:
- prompt_blocks: bfloat16 [256, 2, 128, 1024], P(('groups', 'inst'), None, None, 'tp'), parts along dimension 0, may hold values from -9 to 9
- block_dest: int32 [256], P(('groups', 'inst')), parts along dimension 0, may hold values from 0 to 3, as said below
- block_slot: int32 [256], P(('groups', 'inst')), parts along dimension 0, may hold values from 0 to 63, as said below
- resident_cache: bfloat16 [16, 32, 2, 128, 1024], P(('groups', 'inst'), 'tp'), parts along dimension 0, may hold values from -9 to 9
- queries: bfloat16 [32, 8192], P(('groups', 'inst')), parts along dimension 0, may hold values from -32 to 32
- context_length: int32 [32], P(('groups', 'inst')), parts along dimension 0, may hold values from 1 to 4096, as said below
Outputs:
- attended: bfloat16 [32, 8192], P(('groups', 'inst'), 'tp'), parts along dimension 0
- installed: bfloat16 [16, 32, 2, 128, 1024], P(('groups', 'inst'), 'tp'), parts along dimension 0
There are 2 independent parts, one for each index of `groups`. A program takes and returns all parts, laid end to end along the dimension named above; each array names one. Nothing has to cross between parts.
Inputs may be any that keep to these rules, and one draw needn't show every extreme that they name: `block_dest`: blocks k * 32 to (k + 1) * 32 - 1 are the prompt of instance k. At most 16 blocks of one instance's prompt name the same receiving instance, and in every prompt one receiving instance is named exactly 16 times. `block_slot`: blocks sent to one instance name distinct slots; slot q is page q % 32 of that instance's sequence q // 32. `context_length`: the 2 rows of a sequence are consecutive, their lengths rise by one from step to step, and in every instance one sequence's last row sees all 4096 positions.
All inputs are finite; a program needn't handle non-finite values.
Results may differ from a plain program's by a relative error of at most 0.001.
Values may be sent and summed in bfloat16 or wider, within the bound.
A program may use at most 128 MiB of HBM per device.

v0:
```python
import jax
import jax.numpy as jnp
from jax import lax
from jax.sharding import PartitionSpec as P

H = 64
KVH = 8
HD = 128
STEPS = 2


masked_score = -1e30


def joined(value, axis, join):
    pieces = jax.tree.map(lambda part: lax.all_gather(part, axis), value)
    head = jax.tree.map(lambda part: part[0], pieces)
    tail = jax.tree.map(lambda part: part[1:], pieces)
    subtotal, _ = lax.scan(lambda subtotal, piece: (join(subtotal, piece), None), head, tail)
    return subtotal


def source_ranks(destinations):
    block_total = destinations.shape[-1]
    same_dest = destinations[..., :, None] == destinations[..., None, :]
    earlier = jnp.arange(block_total)[None, :] < jnp.arange(block_total)[:, None]
    return jnp.sum(jnp.logical_and(same_dest, earlier), axis=-1)


def partial_states(grouped, page_rows, usable):
    seq_count = page_rows.shape[0]
    kv_heads = grouped.shape[2]
    head_size = grouped.shape[4]
    split_pages = page_rows.reshape(
        seq_count, page_rows.shape[1], 2, page_rows.shape[3], kv_heads, head_size
    )
    key_rows = split_pages[:, :, 0].reshape(seq_count, -1, kv_heads, head_size)
    value_rows = split_pages[:, :, 1].reshape(seq_count, -1, kv_heads, head_size)
    scores = jnp.einsum(
        "sevgd,skvd->sevgk", grouped, key_rows, preferred_element_type=jnp.float32
    ) * head_size ** (-0.5)
    key_mask = usable[:, :, None, None, :]
    peak = jnp.max(jnp.where(key_mask, scores, masked_score), axis=-1)
    weights = jnp.where(key_mask, jnp.exp(scores - peak[..., None]), 0.0)
    denominator = jnp.sum(weights, axis=-1)
    numerator = jnp.einsum(
        "sevgk,skvd->sevgd",
        weights,
        value_rows.astype(jnp.float32),
        precision=lax.Precision.HIGHEST,
    )
    return (peak, denominator, numerator)


def fold_states(former, latter):
    peak = jnp.maximum(former[0], latter[0])
    former_factor = jnp.exp(former[0] - peak)
    latter_factor = jnp.exp(latter[0] - peak)
    denominator = former[1] * former_factor + latter[1] * latter_factor
    numerator = former[2] * former_factor[..., None] + latter[2] * latter_factor[..., None]
    return (peak, denominator, numerator)


def on_device(prompt_blocks, block_dest, block_slot, resident_cache, queries, context_length):
    inst_count = lax.axis_size("inst")
    tp_count = lax.axis_size("tp")
    my_inst = lax.axis_index("inst")
    my_tp = lax.axis_index("tp")
    block_count = block_dest.shape[0]
    seq_count = resident_cache.shape[0]
    page_local = resident_cache.shape[1]
    pages_seq = page_local * tp_count
    slot_count = seq_count * pages_seq
    capacity = 2 * block_count // inst_count
    block_tok = resident_cache.shape[3]
    rank_of = source_ranks(block_dest)
    target = block_dest * capacity + rank_of
    buffer_pos = jnp.arange(inst_count * capacity, dtype=jnp.int32)
    matches = buffer_pos[:, None] == target[None, :]
    filled = jnp.any(matches, axis=1)
    chosen = jnp.sum(
        jnp.where(matches, jnp.arange(block_count, dtype=jnp.int32)[None, :], 0), axis=1
    )
    outgoing = jnp.where(
        filled[:, None, None, None],
        jnp.take(prompt_blocks, chosen, axis=0),
        jnp.zeros((), prompt_blocks.dtype),
    )
    outgoing = outgoing.reshape((inst_count, capacity) + prompt_blocks.shape[1:])
    arrived = lax.all_to_all(outgoing, "inst", split_axis=0, concat_axis=0, tiled=True)
    arrived = arrived.reshape((inst_count * capacity,) + prompt_blocks.shape[1:])
    every_dest, every_slot = (
        lax.all_gather(block_dest, "inst", axis=0, tiled=True),
        lax.all_gather(block_slot, "inst", axis=0, tiled=True),
    )
    every_rank = source_ranks(every_dest.reshape(inst_count, block_count)).reshape(-1)
    source_of = jnp.arange(inst_count * block_count, dtype=jnp.int32) // block_count
    is_mine = every_dest == my_inst
    wanted = jnp.arange(slot_count, dtype=jnp.int32)
    slot_hit = jnp.logical_and(is_mine[None, :], every_slot[None, :] == wanted[:, None])
    present = jnp.any(slot_hit, axis=1)
    anchor = jnp.sum(jnp.where(slot_hit, (source_of * capacity + every_rank)[None, :], 0), axis=1)
    page_grid = jnp.take(arrived, anchor, axis=0).reshape(
        (seq_count, pages_seq) + arrived.shape[1:]
    )
    delivered = lax.all_to_all(page_grid, "tp", split_axis=1, concat_axis=4, tiled=True)
    own_present = lax.dynamic_slice_in_dim(
        present.reshape(seq_count, pages_seq), my_tp * page_local, page_local, 1
    )
    installed = jnp.where(own_present[:, :, None, None, None], delivered, resident_cache)
    grouped = queries.reshape(seq_count, STEPS, KVH, H // KVH, HD)
    length_rows = context_length.reshape(seq_count, STEPS)
    local_pos = (my_tp * page_local + jnp.arange(page_local, dtype=jnp.int32))[
        :, None
    ] * block_tok + jnp.arange(block_tok, dtype=jnp.int32)[None, :]
    usable = local_pos.reshape(-1)[None, None, :] < length_rows[:, :, None]
    partial_value = partial_states(grouped, installed, usable)
    out_cols = H * HD // tp_count
    combined = joined(partial_value, "tp", fold_states)
    result = (combined[2] / combined[1][..., None]).reshape(seq_count * STEPS, H * HD)
    attended = lax.dynamic_slice_in_dim(result, my_tp * out_cols, out_cols, 1)
    return (attended.astype(jnp.bfloat16), installed)


def solution(mesh):
    in_specs = (
        P(("groups", "inst"), None, None, "tp"),
        P(("groups", "inst")),
        P(("groups", "inst")),
        P(("groups", "inst"), "tp", None, None, None),
        P(("groups", "inst"), None),
        P(("groups", "inst")),
    )
    out_specs = (P(("groups", "inst"), "tp"), P(("groups", "inst"), "tp", None, None, None))
    return jax.shard_map(
        on_device, mesh=mesh, in_specs=in_specs, out_specs=out_specs, check_vma=False
    )
```

profile of v0, /device:TPU:0, one launch (start us, length us, event | category | flops | bytes accessed | tf_op | source)
XLA Modules:
  0.0 432.4 jit_solution(15384231375911069294)
XLA Ops:
  0.6 0.9 convert_reduce_fusion.1
  1.5 0.7 multiply_add_fusion
  2.6 7.8 %gather_fusion = bf16[64,2,128,256]{3,2,1,0:T(8,128)(2,1)} fusion(bf16[32,2,128,256]{3,2,1,0:T(8,128)(2,1)} %param.8, s32[1024]{0:T(1024)S(1)} %pad_clamp_fusion.1), kind=kCustom, calls=%fused_computation | custom fusion | bytes 16777472 | tf_op jit(solution)/shard_map/jit(_take)/gather | solution.py:86
  10.4 7.8 %select_select_fusion = bf16[4,16,2,128,256]{4,3,2,1,0:T(8,128)(2,1)} fusion(bf16[4,16,2,128,256]{4,3,2,1,0:T(8,128)(2,1)} %bitcast.65, pred[4,16]{1,0:T(4,128)(4,1)S(1)} %compare_and_fusion, pred[4,16]{1,0:T(4,128)(4,1)S(1)} %broadcast_in_dim.112), kind=kLoop, calls=%fused_computation.11 | loop fusion | flops 8388608 | bytes 16777344 | tf_op jit(solution)/shard_map/jit(_where)/select_n | solution.py:84
  18.2 5.8 %all-to-all-start = ((bf16[4,16,2,128,256]{4,3,2,1,0:T(8,128)(2,1)}), bf16[4,16,2,128,256]{4,3,2,1,0:T(8,128)(2,1)}, u32[]{:S(2)}, u32[]{:S(2)}) async-start(bf16[4,16,2,128,256]{4,3,2,1,0:T(8,128)(2,1)} %select_select_fusion), calls=%async_computation | async-start | bytes 16777216 | tf_op jit(solution)/shard_map/all_to_all | solution.py:90
  24.0 0.6 dynamic-slice
  25.2 0.2 dynamic-update-slice
  25.5 0.2 dynamic-update-slice.1
  25.7 92.1 %all-reduce.2 = (s32[128]{0:T(128)S(1)}, s32[128]{0:T(128)S(1)}) all-reduce(s32[128]{0:T(128)S(1)} %dynamic-update-slice, s32[128]{0:T(128)S(1)} %dynamic-update-slice.1), channel_id=1, replica_groups=mesh['groups'=2,'inst'=4,'tp'=4] {'inst'}, use_global_device_ids=true, to_apply=%add | all-reduce | flops 256 | bytes 2048
  117.9 0.2 convert_reduce_fusion
  118.5 9.0 %gather_fusion.1 = bf16[64,2,128,256]{3,2,1,0:T(8,128)(2,1)} fusion(bf16[64,2,128,256]{3,2,1,0:T(8,128)(2,1)} %bitcast.8, s32[1024]{0:T(1024)S(1)} %pad_clamp_fusion), kind=kCustom, calls=%fused_computation.1 | custom fusion | bytes 16777472 | tf_op jit(solution)/shard_map/jit(_take)/gather | solution.py:103
  127.5 7.6 %broadcast_select_fusion = bf16[2,32,2,128,256]{4,3,2,1,0:T(8,128)(2,1)} fusion(bf16[2,32,2,128,256]{4,3,2,1,0:T(8,128)(2,1)} %bitcast.64, pred[2,32]{1,0:T(4,128)(4,1)S(1)} %compare_and_fusion.1), kind=kLoop, calls=%fused_computation.12 | loop fusion | flops 4194304 | bytes 16777280 | tf_op jit(solution)/shard_map/jit(_take)/select_n | solution.py:103
  135.1 7.7 %copy.51 = bf16[2,32,2,128,256]{4,3,2,0,1:T(8,128)(2,1)} copy(bf16[2,32,2,128,256]{4,3,2,1,0:T(8,128)(2,1)} %broadcast_select_fusion) | data formatting | bytes 16777216 | tf_op jit(solution)/shard_map/jit(_take)/select_n | solution.py:103
  142.8 5.7 %all-to-all-start.1 = ((bf16[2,32,2,128,256]{4,3,2,0,1:T(8,128)(2,1)}), bf16[2,32,2,128,256]{4,3,2,0,1:T(8,128)(2,1)}, u32[]{:S(2)}, u32[]{:S(2)}) async-start(bf16[2,32,2,128,256]{4,3,2,0,1:T(8,128)(2,1)} %copy.51), calls=%async_computation.1 | async-start | bytes 16777216 | tf_op jit(solution)/shard_map/all_to_all | solution.py:106
  148.7 11.7 %copy.54 = bf16[2,8,2,128,1024]{3,4,2,1,0:T(8,128)(2,1)} copy(bf16[2,8,2,128,1024]{4,3,2,1,0:T(8,128)(2,1)} %param.11) | data formatting | bytes 16777216 | tf_op args[3]
  160.7 171.8 %all-to-all-done.1 = bf16[2,32,2,128,256]{4,3,2,0,1:T(8,128)(2,1)} async-done(((bf16[2,32,2,128,256]{4,3,2,0,1:T(8,128)(2,1)}), bf16[2,32,2,128,256]{4,3,2,0,1:T(8,128)(2,1)}, u32[]{:S(2)}, u32[]{:S(2)}) %all-to-all-start.1) | async-done | bytes 8388640 | tf_op jit(solution)/shard_map/all_to_all | solution.py:106
  332.5 11.7 %copy.53 = bf16[2,8,2,128,4,256]{3,5,4,2,1,0:T(8,128)(2,1)} copy(bf16[2,8,2,128,4,256]{5,3,2,0,1,4:T(8,128)(2,1)} %bitcast.14) | data formatting | bytes 16777216 | tf_op jit(solution)/shard_map/all_to_all | solution.py:106
  344.2 6.5 %bitcast_select_fusion = bf16[2,8,2,128,1024]{3,4,2,1,0:T(8,128)(2,1)S(1)} fusion(bf16[2,8,2,128,1024]{3,4,2,1,0:T(8,128)(2,1)} %copy.54, bf16[2,8,2,128,4,256]{3,5,4,2,1,0:T(8,128)(2,1)} %copy.53, pred[2,8]{1,0:T(4,128)(4,1)S(1)} %constant_dynamic-slice_fusion), kind=kLoop, calls=%fused_computation.10 | loop fusion | flops 4194304 | bytes 25165840 | tf_op jit(solution)/shard_map/jit(_where)/select_n | solution.py:110
  350.7 4.2 fusion.18
  354.9 1.9 copy-done
  356.8 6.3 %copy.65 = bf16[2,8,1,128,8,128]{5,3,1,4,0,2:T(8,128)(2,1)} copy(bf16[2,8,1,128,8,128]{3,5,4,2,1,0:T(8,128)(2,1)} %get-tuple-element.92) | data formatting | bytes 8388608
  363.1 6.2 %copy.66 = bf16[2,8,1,128,8,128]{5,3,1,4,0,2:T(8,128)(2,1)} copy(bf16[2,8,1,128,8,128]{3,5,4,2,1,0:T(8,128)(2,1)} %get-tuple-element.91) | data formatting | bytes 8388608
  369.4 3.5 select_reduce_fusion
  372.8 3.7 convolution_bitcast_fusion
  376.5 16.1 %all-gather.2 = f32[8,2,8,8,128]{4,3,2,1,0:T(8,128)S(1)} all-gather(f32[2,2,8,8,128]{4,3,2,1,0:T(8,128)S(1)} %copy.60), channel_id=4, replica_groups=mesh['groups'=2,'inst'=4,'tp'=4] {'tp'}, dimensions={0}, use_global_device_ids=true | all-gather | bytes 655360 | tf_op jit(solution)/shard_map/all_gather | solution.py:16
  392.6 0.3 fusion.4
  393.0 13.3 %all-gather.1 = f32[8,2,8,8]{3,2,1,0:T(8,128)S(1)} all-gather(f32[2,2,8,8]{3,2,1,0:T(8,128)S(1)} %copy.58), channel_id=3, replica_groups=mesh['groups'=2,'inst'=4,'tp'=4] {'tp'}, dimensions={0}, use_global_device_ids=true | all-gather | bytes 5120 | tf_op jit(solution)/shard_map/all_gather | solution.py:16
  406.3 13.1 %all-gather = f32[8,2,8,8]{3,2,1,0:T(8,128)S(1)} all-gather(f32[2,2,8,8]{3,2,1,0:T(8,128)S(1)} %copy.57), channel_id=2, replica_groups=mesh['groups'=2,'inst'=4,'tp'=4] {'tp'}, dimensions={0}, use_global_device_ids=true | all-gather | bytes 5120 | tf_op jit(solution)/shard_map/all_gather | solution.py:16
  419.4 11.6 %copy.61 = bf16[2,8,2,128,1024]{4,3,2,1,0:T(8,128)(2,1)} copy(bf16[2,8,2,128,1024]{3,4,2,1,0:T(8,128)(2,1)} %copy-done) | data formatting | bytes 16777216
  431.0 0.6 while.14
  431.3 0.2 fusion.24
  431.8 0.6 dynamic-slice_convert_fusion
  (55 shorter events, 1.9 us)
Async XLA Ops:
  18.1 5.8 %copy-start.5 = (u32[32]{0:T(128)S(1)}, u32[32]{0:T(128)}, u32[]{:S(2)}) copy-start(u32[32]{0:T(128)} %constant.92) | copy-start | bytes 388
  18.1 7.1 %copy-start.2 = (s32[32]{0:T(128)S(1)}, s32[32]{0:T(128)}, u32[]{:S(2)}) copy-start(s32[32]{0:T(128)} %param.9) | copy-start | bytes 388
  18.1 7.3 %copy-start.3 = (s32[32]{0:T(128)S(1)}, s32[32]{0:T(128)}, u32[]{:S(2)}) copy-start(s32[32]{0:T(128)} %param.10) | copy-start | bytes 388
  18.2 100.3 %all-to-all-start = ((bf16[4,16,2,128,256]{4,3,2,1,0:T(8,128)(2,1)}), bf16[4,16,2,128,256]{4,3,2,1,0:T(8,128)(2,1)}, u32[]{:S(2)}, u32[]{:S(2)}) async-start(bf16[4,16,2,128,256]{4,3,2,1,0:T(8,128)(2,1)} %select_select_fusion), calls=%async_computation | async-start | bytes 16777216 | tf_op jit(solution)/shard_map/all_to_all | solution.py:90
  142.8 189.7 %all-to-all-start.1 = ((bf16[2,32,2,128,256]{4,3,2,0,1:T(8,128)(2,1)}), bf16[2,32,2,128,256]{4,3,2,0,1:T(8,128)(2,1)}, u32[]{:S(2)}, u32[]{:S(2)}) async-start(bf16[2,32,2,128,256]{4,3,2,0,1:T(8,128)(2,1)} %copy.51), calls=%async_computation.1 | async-start | bytes 16777216 | tf_op jit(solution)/shard_map/all_to_all | solution.py:106
  148.7 11.7 %copy-start.4 = (s32[4]{0:T(128)S(1)}, s32[4]{0:T(128)}, u32[]{:S(2)}) copy-start(s32[4]{0:T(128)} %param.13) | copy-start | bytes 52
  148.7 11.7 %copy-start.1 = (bf16[4,8192]{1,0:T(4,128)(2,1)S(1)}, bf16[4,8192]{1,0:T(4,128)(2,1)}, u32[]{:S(2)}) copy-start(bf16[4,8192]{1,0:T(4,128)(2,1)} %param.12) | copy-start | bytes 196612
  350.7 6.1 %copy-start = (bf16[2,8,2,128,1024]{3,4,2,1,0:T(8,128)(2,1)}, bf16[2,8,2,128,1024]{3,4,2,1,0:T(8,128)(2,1)S(1)}, u32[]{:S(2)}) copy-start(bf16[2,8,2,128,1024]{3,4,2,1,0:T(8,128)(2,1)S(1)} %bitcast_select_fusion) | copy-start | bytes 25165828
where the time goes:
time: 434 us; the launch traced here: 432 us
  waiting for transfers between devices  172 us (40%)
  blocking collectives  135 us (31%)
  local copies, waits for them, and re-layouts  80.5 us (19%)
  other arithmetic  25.4 us (6%)
  starting transfers between devices  11.4 us (3%)
  matrix products  7.13 us (2%)
    all_to_all x1, waiting for transfers between devices, on_device(): lax.all_to_all(page_grid, 'tp', split_axis=1, concat_axis=4, tiled=True)  172 us
    unnamed x1, blocking collectives  92.1 us
    all_gather x3, blocking collectives, joined(): pieces = jax.tree.map(lambda part: lax.all_gather(part, axis), value)  42.5 us
    unnamed x22, local copies, waits for them, and re-layouts  38.8 us
    all_to_all x1, local copies, waits for them, and re-layouts, on_device(): lax.all_to_all(page_grid, 'tp', split_axis=1, concat_axis=4, tiled=True)  11.7 us
    gather x1, local copies, waits for them, and re-layouts, on_device(): jnp.take(arrived, anchor, axis=0)  8.97 us
  transfers between devices with their start and end apart: 2, of which 1 were waited for; matrix products, arithmetic and copies ran while one was open for 3% of the time, Pallas kernels for 0%

commit v1 on v0

v1 whole, which is shorter than its diff:
```python
import functools

import jax
import jax.numpy as jnp
from jax import lax
from jax.experimental import pallas as pl
from jax.experimental.pallas import tpu as pltpu
from jax.sharding import PartitionSpec as P

H = 64
KVH = 8
HD = 128
STEPS = 2
GROUP = H // KVH
CORES = 2
PIECES = 8
MIB = 1024 * 1024

masked_score = -1e30
MESH_ID = pl.DeviceIdType.MESH


def migrate_kernel(
    insts, tps, share, index_ref, prompt_ref, page_ref, packed,
    x_send, x_recv, own_send, own_recv, hop_send, hop_recv,
    z_send, z_recv, back_send, back_recv, local_sem, keep_sem, *gathered,
):
    me = lax.axis_index("inst")
    tp = lax.axis_index("tp")
    core = lax.rem(me, CORES)
    chip = me // CORES
    chips = insts // CORES
    partner = me + 1 - 2 * core
    blocks, rows, width = prompt_ref.shape
    piece = rows // PIECES

    def mirror(step):
        return lax.rem(chip + step, chips) * CORES + core

    def tp_peer(step):
        return lax.rem(tp + step, tps)

    barrier = pltpu.get_barrier_semaphore()
    pl.semaphore_signal(barrier, inc=1, device_id={"inst": partner}, device_id_type=MESH_ID)
    for step in range(1, chips):
        pl.semaphore_signal(barrier, inc=1, device_id={"inst": mirror(step)}, device_id_type=MESH_ID)
    for step in range(1, tps):
        pl.semaphore_signal(barrier, inc=1, device_id={"tp": tp_peer(step)}, device_id_type=MESH_ID)
    pl.semaphore_wait(barrier, chips + tps - 1)

    def span(c):
        return pl.ds(c * piece, piece)

    def remote(src, dst, send, recv, where):
        return pltpu.make_async_remote_copy(
            src_ref=src, dst_ref=dst, send_sem=send, recv_sem=recv,
            device_id=where, device_id_type=MESH_ID,
        )

    def place(inst):
        return pl.ds(inst * blocks, blocks)

    def cross(c):
        src = prompt_ref.at[:, span(c), :]
        dst = gathered[c].at[place(me)]
        return [
            remote(src, dst, x_send.at[c, s - 1], x_recv.at[c, s - 1], {"inst": mirror(s)})
            for s in range(1, chips)
        ]

    def own(c):
        src = prompt_ref.at[:, span(c), :]
        dst = gathered[c].at[place(me)]
        return (
            remote(src, dst, own_send.at[c], own_recv.at[c], {"inst": partner}),
            pltpu.make_async_copy(src, dst, local_sem.at[c]),
        )

    def hop(c, s):
        origin = lax.rem(chip + chips - s, chips) * CORES + core
        part = gathered[c].at[place(origin)]
        return remote(part, part, hop_send.at[c, s - 1], hop_recv.at[c, s - 1], {"inst": partner})

    def spread(c):
        copies = []
        dst = page_ref.at[
            pl.ds(core * share, share), span(c), pl.ds(pl.multiple_of(tp * width, 128), width)
        ]
        for s in range(1, tps):
            peer = tp_peer(s)
            src = packed.at[pl.ds(peer * share, share), span(c), :]
            copies.append(
                remote(src, dst, z_send.at[c, s - 1], z_recv.at[c, s - 1], {"tp": peer})
            )
        kept = packed.at[pl.ds(tp * share, share), span(c), :]
        return copies, pltpu.make_async_copy(kept, dst, keep_sem.at[c])

    def back(c):
        part = page_ref.at[pl.ds(core * share, share), span(c), :]
        return remote(part, part, back_send.at[c], back_recv.at[c], {"inst": partner})

    def begin(c):
        for copy in cross(c):
            copy.start()
        for copy in own(c):
            copy.start()

    def finish_spread(c):
        copies, kept = spread(c)
        for copy in copies:
            copy.wait_recv()
        kept.wait()
        back(c).start()

    begin(0)
    begin(1)
    for c in range(PIECES):
        if c + 2 < PIECES:
            begin(c + 2)
        crossing = cross(c)
        for s in range(1, chips):
            crossing[s - 1].wait_recv()
            hop(c, s).start()
        to_partner, kept = own(c)
        kept.wait()
        to_partner.wait_recv()
        for s in range(1, chips):
            hop(c, s).wait_recv()

        def pack(entry, carry):
            packed[entry, span(c), :] = gathered[c][index_ref[entry]]
            return carry

        lax.fori_loop(0, tps * share, pack, 0)
        copies, kept = spread(c)
        for copy in copies:
            copy.start()
        kept.start()
        if c >= 1:
            finish_spread(c - 1)
    finish_spread(PIECES - 1)
    for c in range(PIECES):
        for copy in cross(c):
            copy.wait_send()
        own(c)[0].wait_send()
        for s in range(1, chips):
            hop(c, s).wait_send()
        for copy in spread(c)[0]:
            copy.wait_send()
        back(c).wait()


def migrate(index, prompt, insts, tps, share, collective_id):
    blocks, rows, width = prompt.shape
    chips = insts // CORES
    dma = pltpu.SemaphoreType.DMA
    return pl.pallas_call(
        functools.partial(migrate_kernel, insts, tps, share),
        out_shape=jax.ShapeDtypeStruct((CORES * share, rows, width * tps), prompt.dtype),
        in_specs=[
            pl.BlockSpec(memory_space=pltpu.SMEM),
            pl.BlockSpec(memory_space=pl.ANY),
        ],
        out_specs=pl.BlockSpec(memory_space=pl.ANY),
        scratch_shapes=[
            pltpu.VMEM((tps * share, rows, width), prompt.dtype),
            dma((PIECES, chips - 1)), dma((PIECES, chips - 1)),
            dma((PIECES,)), dma((PIECES,)),
            dma((PIECES, chips - 1)), dma((PIECES, chips - 1)),
            dma((PIECES, tps - 1)), dma((PIECES, tps - 1)),
            dma((PIECES,)), dma((PIECES,)),
            dma((PIECES,)), dma((PIECES,)),
        ]
        + [pltpu.VMEM((insts * blocks, rows // PIECES, width), prompt.dtype)] * PIECES,
        compiler_params=pltpu.CompilerParams(
            collective_id=collective_id, has_side_effects=True, vmem_limit_bytes=48 * MIB
        ),
        name="migrate",
    )(index, prompt)


def attend_kernel(
    page_local, flag_ref, place_ref, length_ref, base_ref,
    page_ref, resident_ref, query_ref, out_ref, state_ref,
):
    step = pl.program_id(0)
    seq = step // page_local
    page = lax.rem(step, page_local)
    fresh = flag_ref[step] > 0

    @pl.when(fresh)
    def _():
        out_ref[...] = page_ref[...]

    @pl.when(jnp.logical_not(fresh))
    def _():
        out_ref[...] = resident_ref[...]

    @pl.when(page == 0)
    def _():
        state_ref[0, 0] = jnp.full(state_ref.shape[2:], masked_score, jnp.float32)
        state_ref[0, 1] = jnp.zeros(state_ref.shape[2:], jnp.float32)
        state_ref[0, 2] = jnp.zeros(state_ref.shape[2:], jnp.float32)

    tokens = out_ref.shape[1] // 2
    keys = out_ref[0, :tokens, :]
    scores = lax.dot_general(
        query_ref[0], keys, (((1,), (1,)), ((), ())), preferred_element_type=jnp.float32
    ) * HD ** (-0.5)
    row = lax.broadcasted_iota(jnp.int32, scores.shape, 0)
    position = base_ref[0] + page * tokens + lax.broadcasted_iota(jnp.int32, scores.shape, 1)
    decode_step = lax.rem(row // GROUP, STEPS)
    limit = jnp.full(scores.shape, length_ref[seq * STEPS], jnp.int32)
    for e in range(1, STEPS):
        limit = jnp.where(decode_step == e, length_ref[seq * STEPS + e], limit)
    usable = position < limit
    old_peak = state_ref[0, 0]
    best = jnp.max(jnp.where(usable, scores, masked_score), axis=1, keepdims=True)
    peak = jnp.maximum(old_peak, best)
    factor = jnp.exp(old_peak - peak)
    weights = jnp.where(usable, jnp.exp(scores - peak[:, :1]), 0.0)
    state_ref[0, 0] = peak
    state_ref[0, 1] = state_ref[0, 1] * factor + jnp.sum(weights, axis=1, keepdims=True)
    high = weights.astype(jnp.bfloat16)
    low = (weights - high.astype(jnp.float32)).astype(jnp.bfloat16)
    rows = STEPS * GROUP
    for v in range(KVH):
        values = out_ref[0, tokens:, v * HD : (v + 1) * HD]
        part = slice(v * rows, (v + 1) * rows)
        both = jnp.concatenate([high[part], low[part]], axis=0)
        product = jnp.dot(both, values, preferred_element_type=jnp.float32)
        state_ref[0, 2, part, :] = (
            state_ref[0, 2, part, :] * factor[part] + product[:rows] + product[rows:]
        )


def attend(flags, places, lengths, base, pages, resident, queries, seqs):
    total, rows, width = resident.shape
    page_local = total // seqs
    heads = KVH * STEPS * GROUP
    grid_spec = pltpu.PrefetchScalarGridSpec(
        num_scalar_prefetch=4,
        grid=(total,),
        in_specs=[
            pl.BlockSpec((1, rows, width), lambda s, f, p, l, b: (p[s], 0, 0)),
            pl.BlockSpec((1, rows, width), lambda s, f, p, l, b: (s, 0, 0)),
            pl.BlockSpec((1, heads, KVH * HD), lambda s, f, p, l, b: (s // page_local, 0, 0)),
        ],
        out_specs=[
            pl.BlockSpec((1, rows, width), lambda s, f, p, l, b: (s, 0, 0)),
            pl.BlockSpec((1, 3, heads, HD), lambda s, f, p, l, b: (s // page_local, 0, 0, 0)),
        ],
    )
    return pl.pallas_call(
        functools.partial(attend_kernel, page_local),
        grid_spec=grid_spec,
        out_shape=[
            jax.ShapeDtypeStruct(resident.shape, resident.dtype),
            jax.ShapeDtypeStruct((seqs, 3, heads, HD), jnp.float32),
        ],
        compiler_params=pltpu.CompilerParams(vmem_limit_bytes=32 * MIB),
        name="attend",
    )(flags, places, lengths, base, pages, resident, queries)


def combine_kernel(tps, state_ref, out_ref, arrived, send_sem, recv_sem):
    tp = lax.axis_index("tp")
    rows = out_ref.shape[1]
    barrier = pltpu.get_barrier_semaphore()
    for s in range(1, tps):
        pl.semaphore_signal(
            barrier, inc=1, device_id={"tp": lax.rem(tp + s, tps)}, device_id_type=MESH_ID
        )
    pl.semaphore_wait(barrier, tps - 1)
    copies = []
    for s in range(1, tps):
        peer = lax.rem(tp + s, tps)
        copies.append(
            pltpu.make_async_remote_copy(
                src_ref=state_ref.at[:, :, pl.ds(pl.multiple_of(peer * rows, 8), rows), :],
                dst_ref=arrived.at[s - 1],
                send_sem=send_sem.at[s - 1],
                recv_sem=recv_sem.at[s - 1],
                device_id={"tp": peer},
                device_id_type=MESH_ID,
            )
        )
    for copy in copies:
        copy.start()
    mine = state_ref[:, :, pl.ds(pl.multiple_of(tp * rows, 8), rows), :]
    peak, denominator, numerator = mine[:, 0], mine[:, 1], mine[:, 2]
    for s in range(1, tps):
        copies[s - 1].wait()
        other = arrived[s - 1]
        joint = jnp.maximum(peak, other[:, 0])
        here = jnp.exp(peak - joint)
        there = jnp.exp(other[:, 0] - joint)
        denominator = denominator * here + other[:, 1] * there
        numerator = numerator * here + other[:, 2] * there
        peak = joint
    out_ref[...] = (numerator / denominator).astype(out_ref.dtype)


def combine(state, tps):
    seqs, kinds, heads, size = state.shape
    rows = heads // tps
    return pl.pallas_call(
        functools.partial(combine_kernel, tps),
        out_shape=jax.ShapeDtypeStruct((seqs, rows, size), jnp.bfloat16),
        in_specs=[pl.BlockSpec(memory_space=pltpu.VMEM)],
        out_specs=pl.BlockSpec(memory_space=pltpu.VMEM),
        scratch_shapes=[
            pltpu.VMEM((tps - 1, seqs, kinds, rows, size), jnp.float32),
            pltpu.SemaphoreType.DMA((tps - 1,)),
            pltpu.SemaphoreType.DMA((tps - 1,)),
        ],
        compiler_params=pltpu.CompilerParams(collective_id=1, has_side_effects=True),
        name="combine",
    )(state)


def on_device(prompt_blocks, block_dest, block_slot, resident_cache, queries, context_length):
    insts = lax.axis_size("inst")
    tps = lax.axis_size("tp")
    me = lax.axis_index("inst")
    tp = lax.axis_index("tp")
    blocks, kinds, tokens, width = prompt_blocks.shape
    seqs, page_local = resident_cache.shape[:2]
    pages_seq = page_local * tps
    share = seqs * page_local
    every = lax.all_gather(jnp.stack([block_dest, block_slot]), "inst", axis=1, tiled=True)
    dest, slot = every[0], every[1]
    total = insts * blocks
    holder = (slot % pages_seq) // page_local
    pool = (dest // CORES) * tps + holder
    order = jnp.arange(total, dtype=jnp.int32)
    rank = jnp.sum(
        jnp.logical_and(pool[:, None] == pool[None, :], order[None, :] < order[:, None]),
        axis=1,
        dtype=jnp.int32,
    )
    entry = jnp.arange(tps * share, dtype=jnp.int32)
    entry_pool = (me // CORES) * tps + entry // share
    entry_rank = (entry % share) * CORES + me % CORES
    hits = jnp.logical_and(pool[None, :] == entry_pool[:, None], rank[None, :] == entry_rank[:, None])
    index = jnp.sum(jnp.where(hits, order[None, :], 0), axis=1, dtype=jnp.int32)
    local = jnp.arange(share, dtype=jnp.int32)
    wanted = (local // page_local) * pages_seq + tp * page_local + local % page_local
    found = jnp.logical_and(dest[None, :] == me, slot[None, :] == wanted[:, None])
    spot = (rank % CORES) * share + rank // CORES
    places = jnp.sum(jnp.where(found, spot[None, :], 0), axis=1, dtype=jnp.int32)
    flags = jnp.any(found, axis=1).astype(jnp.int32)

    prompt = prompt_blocks.reshape(blocks, kinds * tokens, width)
    pages = migrate(index, prompt, insts, tps, share, 0)

    by_head = queries.reshape(seqs, STEPS, KVH, GROUP, HD).transpose(0, 2, 1, 3, 4)
    by_head = by_head.reshape(seqs, KVH, STEPS * GROUP, 1, HD)
    diagonal = jnp.eye(KVH, dtype=jnp.bool_)[None, :, None, :, None]
    wide = jnp.where(diagonal, by_head, jnp.zeros((), queries.dtype))
    wide = wide.reshape(seqs, KVH * STEPS * GROUP, KVH * HD)
    base = (tp * pages_seq // tps * tokens).astype(jnp.int32).reshape(1)
    resident = resident_cache.reshape(share, kinds * tokens, width * tps)
    installed, state = attend(flags, places, context_length, base, pages, resident, wide, seqs)
    merged = combine(state, tps)
    attended = merged.reshape(seqs, KVH // tps, STEPS, GROUP, HD).transpose(0, 2, 1, 3, 4)
    attended = attended.reshape(seqs * STEPS, H * HD // tps)
    return attended, installed.reshape(resident_cache.shape)


def solution(mesh):
    in_specs = (
        P(("groups", "inst"), None, None, "tp"),
        P(("groups", "inst")),
        P(("groups", "inst")),
        P(("groups", "inst"), "tp", None, None, None),
        P(("groups", "inst"), None),
        P(("groups", "inst")),
    )
    out_specs = (P(("groups", "inst"), "tp"), P(("groups", "inst"), "tp", None, None, None))
    return jax.shard_map(
        on_device, mesh=mesh, in_specs=in_specs, out_specs=out_specs, check_vma=False
    )
```

time: 434 us -> 249 us (0.57)
  Pallas kernels: 0 us -> 234 us
  waiting for transfers between devices: 172 us -> 0 us
  blocking collectives: 135 us -> 5.98 us
  local copies, waits for them, and re-layouts: 80.5 us -> 5.87 us
  other arithmetic: 25.4 us -> 1.56 us
  starting transfers between devices: 11.4 us -> 0 us
  matrix products: 7.13 us -> 0 us
    pallas_call x0 -> x3, Pallas kernels: none -> 234 us  [the longest x1 200 us: migrate(): pl.pallas_call(functools.partial(migrate_kernel, insts, tps, share), out_...]
    all_to_all x2 -> x0, waiting for transfers between devices: 172 us -> none  [the longest x1 172 us: on_device(): lax.all_to_all(page_grid, 'tp', split_axis=1, concat_axis=4, tiled=True)]
    unnamed x1 -> x0, blocking collectives: 92.1 us -> none
    all_gather x3 -> x1, blocking collectives: 42.5 us -> 5.98 us  [on_device(): lax.all_gather(jnp.stack([block_dest, block_slot]), 'inst', axis=1, tiled...]
    unnamed x22 -> x13, local copies, waits for them, and re-layouts: 38.8 us -> 4.09 us
    select_n x5 -> x1, other arithmetic: 22 us -> 0.07 us  [on_device(): wide = jnp.where(diagonal, by_head, jnp.zeros((), queries.dtype))]
    gather x2 -> x0, local copies, waits for them, and re-layouts: 16.7 us -> none  [the longest x1 8.97 us: on_device(): jnp.take(arrived, anchor, axis=0)]
    all_to_all x1 -> x0, local copies, waits for them, and re-layouts: 11.7 us -> none  [on_device(): lax.all_to_all(page_grid, 'tp', split_axis=1, concat_axis=4, tiled=True)]
  transfers between devices with their start and end apart: 2 -> 0, of which waited for: 1 -> 0; matrix products, arithmetic and copies ran while one was open for 3% -> 0% of each run, Pallas kernels for 0% -> 0%
where the time goes in v1:
time: 249 us; the launch traced here: 248 us
  Pallas kernels  234 us (94%)
  blocking collectives  5.98 us (2%)
  local copies, waits for them, and re-layouts  5.87 us (2%)
    pallas_call x1, Pallas kernels, migrate(): pl.pallas_call(functools.partial(migrate_kernel, insts, tps, share), out_...  200 us
    pallas_call x1, Pallas kernels, combine(): pl.pallas_call(functools.partial(combine_kernel, tps), out_shape=jax.Shap...  17.3 us
    pallas_call x1, Pallas kernels, attend(): pl.pallas_call(functools.partial(attend_kernel, page_local), grid_spec=gr...  17 us
    all_gather x1, blocking collectives, on_device(): lax.all_gather(jnp.stack([block_dest, block_slot]), 'inst', axis=1, tiled...  5.98 us

profile of v1, /device:TPU:0, one launch (start us, length us, event | category | flops | bytes accessed | tf_op | source)
XLA Modules:
  0.0 248.4 jit_solution(12687775956051768073)
XLA Ops:
  0.7 0.7 add_bitcast_fusion
  1.4 6.0 %all-gather = s32[4,32,2]{1,2,0:T(2,128)S(1)} all-gather(s32[1,32,2]{1,2,0:T(2,128)S(1)} %add_bitcast_fusion), channel_id=1, replica_groups=mesh['groups'=2,'inst'=4,'tp'=4] {'inst'}, dimensions={0}, use_global_device_ids=true | all-gather | bytes 1280 | tf_op jit(solution)/shard_map/all_gather | solution.py:331
  7.4 0.1 reshape.190
  7.5 0.2 convert_reduce_fusion
  7.7 0.2 select_reduce_fusion.index_ref
  7.9 0.2 select_reduce_fusion.1.place_ref
  8.1 0.2 fusion.1
  8.3 0.9 copy.21
  9.1 0.1 broadcast_in_dim.68
  9.3 0.1 copy.24
  9.3 0.1 broadcast_in_dim.72
  9.4 0.2 broadcast_in_dim.73
  9.7 0.0 slice-start
  9.7 0.1 broadcast_select_fusion.query_ref
  9.7 0.0 copy-start
  9.8 2.3 copy-done
  12.1 0.0 slice-start.1
  12.1 0.0 copy-start.2
  12.1 199.8 %migrate.1.page_ref = bf16[32,256,1024]{2,1,0:T(8,128)(2,1)} custom-call(s32[64]{0:T(128)S(1)} %select_reduce_fusion.index_ref, bf16[32,256,256]{2,1,0:T(8,128)(2,1)S(1)} %bitcast.54), custom_call_target="tpu_custom_call" | custom-call | tf_op jit(solution)/shard_map/migrate/pallas_call | solution.py:157
  211.9 0.0 slice-done
  211.9 0.0 slice-done.1
  212.0 0.0 copy-done.2
  212.0 17.0 %attend.1 = (bf16[16,256,1024]{2,1,0:T(8,128)(2,1)}, f32[2,3,128,128]{3,2,1,0:T(8,128)S(1)}) custom-call(s32[16]{0:T(128)S(1)} %convert_element_type.6.flag_ref, s32[16]{0:T(128)S(1)} %select_reduce_fusion.1.place_ref, s32[4]{0:T(128)S(1)} %copy-done.2, s32[1]{0:T(128)} %bitcast.9.base_ref, bf16[32,256,1024]{2,1,0:T(8,128)(2,1)} %migrate.1.page_ref, ...), custom_call_target="tpu_custom_call" | custom-call | tf_op jit(solution)/shard_map/attend/pallas_call | solution.py:254
  229.0 0.0 copy-start.1
  229.0 0.7 copy-done.1
  229.7 17.3 %combine.1 = bf16[2,32,128]{2,1,0:T(8,128)(2,1)} custom-call(f32[2,3,128,128]{3,2,1,0:T(8,128)} %copy-done.1), custom_call_target="tpu_custom_call" | custom-call | tf_op jit(solution)/shard_map/combine/pallas_call | solution.py:307
  247.1 0.7 copy.19
  247.8 0.6 reshape.187
  (11 shorter events, 0.1 us)
Async XLA Ops:
  9.7 202.3 %slice-start = ((s8[8388608]{0:T(1024)(128)(4,1)}), s8[4194304]{0:T(1024)(128)(4,1)S(1)}, s32[]{:S(2)}) async-start(s8[8388608]{0:T(1024)(128)(4,1)} %bitcast.51), calls=%async_computation | async-start | bytes 8388608
  9.7 2.3 copy-start
  12.1 199.9 %slice-start.1 = ((s8[8388608]{0:T(1024)(128)(4,1)}), s8[4194304]{0:T(1024)(128)(4,1)S(1)}, s32[]{:S(2)}) async-start(s8[8388608]{0:T(1024)(128)(4,1)} %bitcast.51), calls=%async_computation.1 | async-start | bytes 8388608
  12.1 199.9 %copy-start.2 = (s32[4]{0:T(128)S(1)}, s32[4]{0:T(128)}, u32[]{:S(2)}) copy-start(s32[4]{0:T(128)} %length_ref.1) | copy-start | bytes 52
  229.0 0.7 copy-start.1

commit v2 on v1

v2 whole, which is shorter than its diff:
```python
import functools

import jax
import jax.numpy as jnp
from jax import lax
from jax.experimental import pallas as pl
from jax.experimental.pallas import tpu as pltpu
from jax.sharding import PartitionSpec as P

H = 64
KVH = 8
HD = 128
STEPS = 2
GROUP = H // KVH
CORES = 2
PARTS = (1, 1, 2, 2, 2, 2, 2, 2, 1, 1)
PIECES = len(PARTS)
LEVELS = (11, 12, 13, 16)
PAGES_STEP = 4
LANES = 128
MIB = 1024 * 1024

masked_score = -1e30
MESH_ID = pl.DeviceIdType.MESH


def migrate_kernel(
    insts, tps, share, sent, index_ref, prompt_ref, page_ref, packed,
    x_send, x_recv, own_send, own_recv, hop_send, hop_recv,
    z_send, z_recv, back_send, back_recv, local_sem, keep_sem, *gathered,
):
    me = lax.axis_index("inst")
    tp = lax.axis_index("tp")
    core = lax.rem(me, CORES)
    chip = me // CORES
    chips = insts // CORES
    partner = me + 1 - 2 * core
    blocks, rows, width = prompt_ref.shape
    unit = rows // sum(PARTS)

    def mirror(step):
        return lax.rem(chip + step, chips) * CORES + core

    def tp_peer(step):
        return lax.rem(tp + step, tps)

    barrier = pltpu.get_barrier_semaphore()
    pl.semaphore_signal(barrier, inc=1, device_id={"inst": partner}, device_id_type=MESH_ID)
    for step in range(1, chips):
        pl.semaphore_signal(barrier, inc=1, device_id={"inst": mirror(step)}, device_id_type=MESH_ID)
    for step in range(1, tps):
        pl.semaphore_signal(barrier, inc=1, device_id={"tp": tp_peer(step)}, device_id_type=MESH_ID)
    pl.semaphore_wait(barrier, chips + tps - 1)

    def span(c):
        return pl.ds(sum(PARTS[:c]) * unit, PARTS[c] * unit)

    def remote(src, dst, send, recv, where):
        return pltpu.make_async_remote_copy(
            src_ref=src, dst_ref=dst, send_sem=send, recv_sem=recv,
            device_id=where, device_id_type=MESH_ID,
        )

    def place(inst):
        return pl.ds(inst * blocks, blocks)

    def cross(c):
        src = prompt_ref.at[:, span(c), :]
        dst = gathered[c].at[place(me)]
        return [
            remote(src, dst, x_send.at[c, s - 1], x_recv.at[c, s - 1], {"inst": mirror(s)})
            for s in range(1, chips)
        ]

    def own(c):
        src = prompt_ref.at[:, span(c), :]
        dst = gathered[c].at[place(me)]
        return (
            remote(src, dst, own_send.at[c], own_recv.at[c], {"inst": partner}),
            pltpu.make_async_copy(src, dst, local_sem.at[c]),
        )

    def hop(c, s):
        origin = lax.rem(chip + chips - s, chips) * CORES + core
        part = gathered[c].at[place(origin)]
        return remote(part, part, hop_send.at[c, s - 1], hop_recv.at[c, s - 1], {"inst": partner})

    def spread(c):
        copies = []
        dst = page_ref.at[
            pl.ds(core * share, sent), span(c), pl.ds(pl.multiple_of(tp * width, 128), width)
        ]
        for s in range(1, tps):
            peer = tp_peer(s)
            src = packed.at[pl.ds(peer * sent, sent), span(c), :]
            copies.append(
                remote(src, dst, z_send.at[c, s - 1], z_recv.at[c, s - 1], {"tp": peer})
            )
        kept = packed.at[pl.ds(tp * sent, sent), span(c), :]
        return copies, pltpu.make_async_copy(kept, dst, keep_sem.at[c])

    def back(c):
        part = page_ref.at[pl.ds(core * share, sent), span(c), :]
        return remote(part, part, back_send.at[c], back_recv.at[c], {"inst": partner})

    def begin(c):
        for copy in cross(c):
            copy.start()
        for copy in own(c):
            copy.start()

    def finish_spread(c):
        copies, kept = spread(c)
        for copy in copies:
            copy.wait_recv()
        kept.wait()
        back(c).start()

    begin(0)
    begin(1)
    for c in range(PIECES):
        if c + 2 < PIECES:
            begin(c + 2)
        crossing = cross(c)
        for s in range(1, chips):
            crossing[s - 1].wait_recv()
            hop(c, s).start()
        to_partner, kept = own(c)
        kept.wait()
        to_partner.wait_recv()
        for s in range(1, chips):
            hop(c, s).wait_recv()

        def pack(entry, carry):
            chosen = index_ref[entry // sent * share + lax.rem(entry, sent)]
            packed[entry, span(c), :] = gathered[c][chosen]
            return carry

        lax.fori_loop(0, tps * sent, pack, 0)
        copies, kept = spread(c)
        for copy in copies:
            copy.start()
        kept.start()
        if c >= 1:
            finish_spread(c - 1)
    finish_spread(PIECES - 1)
    for c in range(PIECES):
        for copy in cross(c):
            copy.wait_send()
        own(c)[0].wait_send()
        for s in range(1, chips):
            hop(c, s).wait_send()
        for copy in spread(c)[0]:
            copy.wait_send()
        back(c).wait()


def migrate(insts, tps, share, sent, collective_id, index, prompt):
    blocks, rows, width = prompt.shape
    chips = insts // CORES
    dma = pltpu.SemaphoreType.DMA
    return pl.pallas_call(
        functools.partial(migrate_kernel, insts, tps, share, sent),
        out_shape=jax.ShapeDtypeStruct((CORES * share, rows, width * tps), prompt.dtype),
        in_specs=[
            pl.BlockSpec(memory_space=pltpu.SMEM),
            pl.BlockSpec(memory_space=pl.ANY),
        ],
        out_specs=pl.BlockSpec(memory_space=pl.ANY),
        scratch_shapes=[
            pltpu.VMEM((tps * sent, rows, width), prompt.dtype),
            dma((PIECES, chips - 1)), dma((PIECES, chips - 1)),
            dma((PIECES,)), dma((PIECES,)),
            dma((PIECES, chips - 1)), dma((PIECES, chips - 1)),
            dma((PIECES, tps - 1)), dma((PIECES, tps - 1)),
            dma((PIECES,)), dma((PIECES,)),
            dma((PIECES,)), dma((PIECES,)),
        ]
        + [
            pltpu.VMEM((insts * blocks, rows // sum(PARTS) * part, width), prompt.dtype)
            for part in PARTS
        ],
        compiler_params=pltpu.CompilerParams(
            collective_id=collective_id, has_side_effects=True, vmem_limit_bytes=48 * MIB
        ),
        name=f"migrate_{sent}",
    )(index, prompt)


def attend_kernel(page_local, flag_ref, place_ref, kept_ref, length_ref, base_ref, *refs):
    pages, residents = refs[:PAGES_STEP], refs[PAGES_STEP : 2 * PAGES_STEP]
    query_ref, out_ref, numerator_ref, stat_ref, peak_ref, denominator_ref = refs[2 * PAGES_STEP :]
    step = pl.program_id(0)
    seq = step * PAGES_STEP // page_local
    first = lax.rem(step * PAGES_STEP, page_local)

    for i in range(PAGES_STEP):
        fresh = flag_ref[step * PAGES_STEP + i] > 0

        @pl.when(fresh)
        def _():
            out_ref[i] = pages[i][0]

        @pl.when(jnp.logical_not(fresh))
        def _():
            out_ref[i] = residents[i][0]

    @pl.when(first == 0)
    def _():
        peak_ref[...] = jnp.full(peak_ref.shape, masked_score, jnp.float32)
        denominator_ref[...] = jnp.zeros(denominator_ref.shape, jnp.float32)
        numerator_ref[...] = jnp.zeros(numerator_ref.shape, jnp.float32)

    tokens = out_ref.shape[1] // 2
    scores = jnp.concatenate(
        [
            lax.dot_general(
                query_ref[0],
                out_ref[i, :tokens, :],
                (((1,), (1,)), ((), ())),
                preferred_element_type=jnp.float32,
            )
            for i in range(PAGES_STEP)
        ],
        axis=1,
    ) * HD ** (-0.5)
    row = lax.broadcasted_iota(jnp.int32, scores.shape, 0)
    start = base_ref[0] + first * tokens
    position = start + lax.broadcasted_iota(jnp.int32, scores.shape, 1)
    decode_step = lax.rem(row // GROUP, STEPS)
    limit = jnp.full(scores.shape, length_ref[seq * STEPS], jnp.int32)
    for e in range(1, STEPS):
        limit = jnp.where(decode_step == e, length_ref[seq * STEPS + e], limit)
    usable = position < limit
    old_peak = peak_ref[...]
    best = jnp.max(jnp.where(usable, scores, masked_score), axis=1, keepdims=True)
    peak = jnp.maximum(old_peak, best)
    factor = jnp.exp(old_peak - peak)
    weights = jnp.where(usable, jnp.exp(scores - peak[:, :1]), 0.0)
    denominator = denominator_ref[...] * factor + jnp.sum(weights, axis=1, keepdims=True)
    peak_ref[...] = peak
    denominator_ref[...] = denominator
    high = weights.astype(jnp.bfloat16)
    low = (weights - high.astype(jnp.float32)).astype(jnp.bfloat16)
    rows = STEPS * GROUP
    for v in range(KVH):
        part = slice(v * rows, (v + 1) * rows)
        both = jnp.concatenate([high[part], low[part]], axis=0)
        product = sum(
            jnp.dot(
                both[:, i * tokens : (i + 1) * tokens],
                out_ref[i, tokens:, v * HD : (v + 1) * HD],
                preferred_element_type=jnp.float32,
            )
            for i in range(PAGES_STEP)
        )
        numerator_ref[0, part, :] = (
            numerator_ref[0, part, :] * factor[part] + product[:rows] + product[rows:]
        )

    @pl.when(first == page_local - PAGES_STEP)
    def _():
        lane = lax.broadcasted_iota(jnp.int32, stat_ref.shape, 1)
        spot = lane // (LANES // 4)
        stats = jnp.where(spot == 2 * seq, peak, stat_ref[...])
        stat_ref[...] = jnp.where(spot == 2 * seq + 1, denominator, stats)


def attend(flags, places, kept, lengths, base, pages, resident, queries, seqs):
    total, rows, width = resident.shape
    page_local = total // seqs
    heads = KVH * STEPS * GROUP
    steps_seq = page_local // PAGES_STEP

    def page_spec(which, i):
        return pl.BlockSpec(
            (1, rows, width), lambda s, *scalars: (scalars[which][s * PAGES_STEP + i], 0, 0)
        )

    grid_spec = pltpu.PrefetchScalarGridSpec(
        num_scalar_prefetch=5,
        grid=(total // PAGES_STEP,),
        in_specs=[page_spec(1, i) for i in range(PAGES_STEP)]
        + [page_spec(2, i) for i in range(PAGES_STEP)]
        + [pl.BlockSpec((1, heads, KVH * HD), lambda s, *scalars: (s // steps_seq, 0, 0))],
        out_specs=[
            pl.BlockSpec((PAGES_STEP, rows, width), lambda s, *scalars: (s, 0, 0)),
            pl.BlockSpec((1, heads, HD), lambda s, *scalars: (s // steps_seq, 0, 0)),
            pl.BlockSpec((heads, LANES), lambda s, *scalars: (0, 0)),
        ],
        scratch_shapes=[pltpu.VMEM((heads, LANES), jnp.float32)] * 2,
    )
    return pl.pallas_call(
        functools.partial(attend_kernel, page_local),
        grid_spec=grid_spec,
        out_shape=[
            jax.ShapeDtypeStruct(resident.shape, resident.dtype),
            jax.ShapeDtypeStruct((seqs, heads, HD), jnp.float32),
            jax.ShapeDtypeStruct((heads, LANES), jnp.float32),
        ],
        compiler_params=pltpu.CompilerParams(vmem_limit_bytes=40 * MIB),
        name="attend",
    )(
        flags, places, kept, lengths, base,
        *[pages] * PAGES_STEP, *[resident] * PAGES_STEP, queries,
    )


def combine_kernel(tps, numerator_ref, stat_ref, out_ref, arrived, arrived_stat, send_sem, recv_sem):
    tp = lax.axis_index("tp")
    seqs, rows = out_ref.shape[:2]
    barrier = pltpu.get_barrier_semaphore()
    for s in range(1, tps):
        pl.semaphore_signal(
            barrier, inc=1, device_id={"tp": lax.rem(tp + s, tps)}, device_id_type=MESH_ID
        )
    pl.semaphore_wait(barrier, tps - 1)
    copies = []
    for s in range(1, tps):
        peer = lax.rem(tp + s, tps)
        part = pl.ds(pl.multiple_of(peer * rows, 8), rows)
        for kind, (src, dst) in enumerate(
            ((numerator_ref.at[:, part, :], arrived), (stat_ref.at[part, :], arrived_stat))
        ):
            copies.append(
                pltpu.make_async_remote_copy(
                    src_ref=src,
                    dst_ref=dst.at[s - 1],
                    send_sem=send_sem.at[kind, s - 1],
                    recv_sem=recv_sem.at[kind, s - 1],
                    device_id={"tp": peer},
                    device_id_type=MESH_ID,
                )
            )
    for copy in copies:
        copy.start()
    mine = pl.ds(pl.multiple_of(tp * rows, 8), rows)
    step = LANES // 4
    for copy in copies:
        copy.wait()
    for seq in range(seqs):
        stats = [stat_ref[mine, :]] + [arrived_stat[s] for s in range(tps - 1)]
        tops = [numerator_ref[seq, mine, :]] + [arrived[s, seq] for s in range(tps - 1)]
        peaks = [part[:, 2 * seq * step : 2 * seq * step + 1] for part in stats]
        lows = [part[:, (2 * seq + 1) * step : (2 * seq + 1) * step + 1] for part in stats]
        peak = functools.reduce(jnp.maximum, peaks)
        factors = [jnp.exp(part - peak) for part in peaks]
        numerator = sum(top * factor for top, factor in zip(tops, factors))
        denominator = sum(low * factor for low, factor in zip(lows, factors))
        out_ref[seq] = (numerator / denominator).astype(out_ref.dtype)


def combine(numerator, stats, tps, collective_id):
    seqs, heads, size = numerator.shape
    rows = heads // tps
    return pl.pallas_call(
        functools.partial(combine_kernel, tps),
        out_shape=jax.ShapeDtypeStruct((seqs, rows, size), jnp.bfloat16),
        in_specs=[pl.BlockSpec(memory_space=pltpu.VMEM)] * 2,
        out_specs=pl.BlockSpec(memory_space=pltpu.VMEM),
        scratch_shapes=[
            pltpu.VMEM((tps - 1, seqs, rows, size), jnp.float32),
            pltpu.VMEM((tps - 1, rows, LANES), jnp.float32),
            pltpu.SemaphoreType.DMA((2, tps - 1)),
            pltpu.SemaphoreType.DMA((2, tps - 1)),
        ],
        compiler_params=pltpu.CompilerParams(collective_id=collective_id, has_side_effects=True),
        name="combine",
    )(numerator, stats)


def on_device(prompt_blocks, block_dest, block_slot, resident_cache, queries, context_length):
    insts = lax.axis_size("inst")
    tps = lax.axis_size("tp")
    me = lax.axis_index("inst")
    tp = lax.axis_index("tp")
    blocks, kinds, tokens, width = prompt_blocks.shape
    seqs, page_local = resident_cache.shape[:2]
    pages_seq = page_local * tps
    share = seqs * page_local
    pairs = lax.all_gather(jnp.stack([block_dest, block_slot]), ("groups", "inst"))
    pairs = pairs.reshape((-1, insts) + pairs.shape[1:]).transpose(0, 2, 1, 3)
    pairs = pairs.reshape(pairs.shape[0], 2, insts * blocks)
    load = pairs[:, 0] // CORES * tps + pairs[:, 1] % pages_seq // page_local
    pools = jnp.arange(insts // CORES * tps, dtype=jnp.int32)
    counts = jnp.sum(load[:, :, None] == pools, axis=1, dtype=jnp.int32)
    needed = (jnp.max(counts) + CORES - 1) // CORES
    every = lax.dynamic_index_in_dim(pairs, lax.axis_index("groups"), 0, keepdims=False)
    dest, slot = every[0], every[1]
    total = insts * blocks
    holder = (slot % pages_seq) // page_local
    pool = (dest // CORES) * tps + holder
    order = jnp.arange(total, dtype=jnp.int32)
    rank = jnp.sum(
        jnp.logical_and(pool[:, None] == pool[None, :], order[None, :] < order[:, None]),
        axis=1,
        dtype=jnp.int32,
    )
    entry = jnp.arange(tps * share, dtype=jnp.int32)
    entry_pool = (me // CORES) * tps + entry // share
    entry_rank = (entry % share) * CORES + me % CORES
    hits = jnp.logical_and(pool[None, :] == entry_pool[:, None], rank[None, :] == entry_rank[:, None])
    index = jnp.sum(jnp.where(hits, order[None, :], 0), axis=1, dtype=jnp.int32)
    local = jnp.arange(share, dtype=jnp.int32)
    wanted = (local // page_local) * pages_seq + tp * page_local + local % page_local
    found = jnp.logical_and(dest[None, :] == me, slot[None, :] == wanted[:, None])
    spot = (rank % CORES) * share + rank // CORES
    places = jnp.sum(jnp.where(found, spot[None, :], 0), axis=1, dtype=jnp.int32)
    flags = jnp.any(found, axis=1).astype(jnp.int32)

    prompt = prompt_blocks.reshape(blocks, kinds * tokens, width)
    levels = sorted({-(-share * level // LEVELS[-1]) for level in LEVELS})
    variant = sum((needed > level).astype(jnp.int32) for level in levels[:-1])
    pages = lax.switch(
        variant,
        [
            functools.partial(migrate, insts, tps, share, sent, i)
            for i, sent in enumerate(levels)
        ],
        index,
        prompt,
    )
    place_rows, kept_rows = [], []
    place_now = kept_now = jnp.zeros((PAGES_STEP,), jnp.int32)
    for row in range(share // PAGES_STEP):
        part = slice(row * PAGES_STEP, (row + 1) * PAGES_STEP)
        fresh = flags[part] > 0
        place_now = jnp.where(fresh, places[part], place_now)
        kept_now = jnp.where(fresh, kept_now, local[part])
        place_rows.append(place_now)
        kept_rows.append(kept_now)
    places, kept = jnp.concatenate(place_rows), jnp.concatenate(kept_rows)

    by_head = queries.reshape(seqs, STEPS, KVH, GROUP, HD).transpose(0, 2, 1, 3, 4)
    by_head = by_head.reshape(seqs, KVH, STEPS * GROUP, 1, HD)
    diagonal = jnp.eye(KVH, dtype=jnp.bool_)[None, :, None, :, None]
    wide = jnp.where(diagonal, by_head, jnp.zeros((), queries.dtype))
    wide = wide.reshape(seqs, KVH * STEPS * GROUP, KVH * HD)
    base = (tp * pages_seq // tps * tokens).astype(jnp.int32).reshape(1)
    resident = resident_cache.reshape(share, kinds * tokens, width * tps)
    installed, numerator, stats = attend(
        flags, places, kept, context_length, base, pages, resident, wide, seqs
    )
    merged = combine(numerator, stats, tps, len(levels))
    attended = merged.reshape(seqs, KVH // tps, STEPS, GROUP, HD).transpose(0, 2, 1, 3, 4)
    attended = attended.reshape(seqs * STEPS, H * HD // tps)
    return attended, installed.reshape(resident_cache.shape)


def solution(mesh):
    in_specs = (
        P(("groups", "inst"), None, None, "tp"),
        P(("groups", "inst")),
        P(("groups", "inst")),
        P(("groups", "inst"), "tp", None, None, None),
        P(("groups", "inst"), None),
        P(("groups", "inst")),
    )
    out_specs = (P(("groups", "inst"), "tp"), P(("groups", "inst"), "tp", None, None, None))
    return jax.shard_map(
        on_device, mesh=mesh, in_specs=in_specs, out_specs=out_specs, check_vma=False
    )
```

time: 249 us -> 186 us (0.75)
  Pallas kernels: 234 us -> 165 us
  blocking collectives: 5.98 us -> 10.3 us
    pallas_call x1, Pallas kernels: 200 us -> 146 us  [migrate(): pl.pallas_call(functools.partial(migrate_kernel, insts, tps, share, sent)...]
    pallas_call x1, Pallas kernels: 17.3 us -> 9.38 us  [combine(): pl.pallas_call(functools.partial(combine_kernel, tps), out_shape=jax.Shap...]
    pallas_call x1, Pallas kernels: 17 us -> 9.64 us  [attend(): pl.pallas_call(functools.partial(attend_kernel, page_local), grid_spec=gr...]
    all_gather x1, blocking collectives: 5.98 us -> 10.3 us  [on_device(): lax.all_gather(jnp.stack([block_dest, block_slot]), ('groups', 'inst'))]
where the time goes in v2:
time: 186 us
  Pallas kernels  165 us (89%)
  blocking collectives  10.3 us (6%)
  local copies, waits for them, and re-layouts  6.61 us (4%)
  other arithmetic  2.5 us (1%)
    pallas_call x1, Pallas kernels, migrate(): pl.pallas_call(functools.partial(migrate_kernel, insts, tps, share, sent)...  146 us
    all_gather x1, blocking collectives, on_device(): lax.all_gather(jnp.stack([block_dest, block_slot]), ('groups', 'inst'))  10.3 us
    pallas_call x1, Pallas kernels, attend(): pl.pallas_call(functools.partial(attend_kernel, page_local), grid_spec=gr...  9.64 us
    pallas_call x1, Pallas kernels, combine(): pl.pallas_call(functools.partial(combine_kernel, tps), out_shape=jax.Shap...  9.38 us
    unnamed x12, local copies, waits for them, and re-layouts  4.72 us

profile of v2, /device:TPU:0, one launch (start us, length us, event | category | flops | bytes accessed | tf_op | source)
XLA Modules:
  0.0 185.5 jit_solution(1949397637047357990)
XLA Ops:
  0.6 0.7 add_bitcast_fusion
  1.3 10.3 %all-gather.1 = s32[8,2,32]{2,1,0:T(2,128)S(1)} all-gather(s32[1,2,32]{2,1,0:T(2,128)S(1)} %add_bitcast_fusion), channel_id=2, replica_groups=mesh['groups'=2,'inst'=4,'tp'=4] {'groups','inst'}, dimensions={0}, use_global_device_ids=true | all-gather | bytes 2304 | tf_op jit(solution)/shard_map/all_gather | solution.py:381
  11.6 0.1 reshape.333
  11.8 0.2 fusion.1
  12.0 0.2 convert_reduce_fusion
  12.2 0.2 select_reduce_fusion.1
  12.4 0.1 compare_select_fusion.13
  12.5 0.1 pad_add_fusion
  12.6 0.1 convert_reduce_fusion.1
  12.7 0.6 reduce_max.9
  14.1 0.2 select_reduce_fusion
  14.3 0.0 copy-start.4
  14.3 0.0 copy-start.3
  14.3 145.5 %conditional.1 = (bf16[32,256,1024]{2,1,0:T(8,128)(2,1)}) conditional(s32[]{:T(128)} %clamp.3, (s32[64]{0:T(128)S(1)}, bf16[32,256,256]{2,1,0:T(8,128)(2,1)}) %tuple.39, (s32[64]{0:T(128)S(1)}, bf16[32,256,256]{2,1,0:T(8,128)(2,1)}) %tuple.40, (s32[64]{0:T(128)S(1)}, bf16[32,256,256]{2,1,0:T(8,128)(2,1)}) %tuple.41, ...), branch_computations={%region_6.7_spmd, %region_7.8_spmd, %region_8.9_spmd, %region_9.10... | conditional | bytes 8 | solution.py:414
  14.3 145.5 %migrate_11.1 = bf16[32,256,1024]{2,1,0:T(8,128)(2,1)} custom-call(s32[64]{0:T(128)S(1)} %get-tuple-element.18.index_ref, bf16[32,256,256]{2,1,0:T(8,128)(2,1)} %get-tuple-element.19.prompt_ref), custom_call_target="tpu_custom_call" | custom-call | tf_op jit(solution)/shard_map/cond/branch_0_fun/migrate_11/pallas_call | solution.py:162
  159.9 0.0 copy-done.4
  159.9 0.1 broadcast_in_dim.74
  160.0 0.2 broadcast_in_dim.75
  160.3 0.1 broadcast_in_dim.70
  160.4 0.1 copy.31
  160.4 0.1 broadcast_select_fusion.refs_8_
  160.5 0.0 copy-done.3
  160.5 0.0 copy-start
  160.5 3.4 %copy-done = bf16[2,8,2,128,1024]{4,3,2,1,0:T(8,128)(2,1)S(1)} copy-done((bf16[2,8,2,128,1024]{4,3,2,1,0:T(8,128)(2,1)S(1)}, bf16[2,8,2,128,1024]{4,3,2,1,0:T(8,128)(2,1)}, u32[]{:S(2)}) %copy-start) | copy-done | bytes 8388632
  163.9 9.6 %attend.1 = (bf16[16,256,1024]{2,1,0:T(8,128)(2,1)}, f32[2,128,128]{2,1,0:T(8,128)S(1)}, f32[128,128]{1,0:T(8,128)S(1)}) custom-call(s32[16]{0:T(128)S(1)} %convert_element_type.18.flag_ref, s32[16]{0:T(128)S(1)} %get-tuple-element.51.place_ref, s32[16]{0:T(128)S(1)} %get-tuple-element.52.kept_ref, s32[4]{0:T(128)S(1)} %copy-done.3, s32[1]{0:T(128)} %bitcast.7.base_ref, ...), custom_call_target="tpu_custom_call" | custom-call | tf_op jit(solution)/shard_map/attend/pallas_call | solution.py:293
  173.5 0.0 copy-start.1
  173.5 0.6 copy-done.1
  174.2 0.0 copy-start.2
  174.2 0.6 copy-done.2
  174.8 9.4 %combine.1 = bf16[2,32,128]{2,1,0:T(8,128)(2,1)} custom-call(f32[2,128,128]{2,1,0:T(8,128)} %copy-done.1, f32[128,128]{1,0:T(8,128)} %copy-done.2), custom_call_target="tpu_custom_call" | custom-call | tf_op jit(solution)/shard_map/combine/pallas_call | solution.py:356
  184.2 0.7 copy.25
  184.9 0.6 reshape.339
  (18 shorter events, 0.1 us)
Async XLA Ops:
  14.3 145.6 %copy-start.4 = (bf16[4,8192]{1,0:T(4,128)(2,1)S(1)}, bf16[4,8192]{1,0:T(4,128)(2,1)}, u32[]{:S(2)}) copy-start(bf16[4,8192]{1,0:T(4,128)(2,1)} %param.14) | copy-start | bytes 196612
  14.3 146.2 %copy-start.3 = (s32[4]{0:T(128)S(1)}, s32[4]{0:T(128)}, u32[]{:S(2)}) copy-start(s32[4]{0:T(128)} %length_ref.1) | copy-start | bytes 52
  160.5 3.4 %copy-start = (bf16[2,8,2,128,1024]{4,3,2,1,0:T(8,128)(2,1)S(1)}, bf16[2,8,2,128,1024]{4,3,2,1,0:T(8,128)(2,1)}, u32[]{:S(2)}) copy-start(bf16[2,8,2,128,1024]{4,3,2,1,0:T(8,128)(2,1)} %param.13) | copy-start | bytes 25165828
  173.5 0.6 copy-start.1
  174.2 0.6 copy-start.2
